TPU v7x, 256 devices: a whole 4x4x8 slice. The times are simulated.
256 devices in a mesh: rows: 64 (over z, x, core), cols: 4 (over y).
Axes of the slice: x: 4, y: 4, z: 8, core: 2. Of those that a mesh axis runs over, the one named last changes fastest.
Arguments:
- vectors: bfloat16 [64, 1048576], P('cols', 'rows'), may hold values from -110 to 110
- tile_vals: bfloat16 [12288, 256, 256], P('rows'), may hold values from -0.21875 to 0.21875
- tile_row: int32 [64, 192], P('rows'), may hold values from 0 to 63
- tile_src: int32 [64, 192], P('rows'), may hold values from 0 to 191, each once within a row
- send_list: int32 [4096, 2], P('rows'), may hold values from 0 to 63
- ritz_matrix: bfloat16 [64, 64], P(None, 'cols'), may hold values from -0.75 to 0.75
Outputs:
- rotated: bfloat16 [64, 1048576], P('cols', 'rows')
- gram_matrix: float32 [64, 64], P('cols')
- projected: float32 [64, 64], P('cols')
Inputs may be any that keep to these rules, and one draw needn't show every extreme that they name: Each row of tile_src holds every number once, so that each own or received block is read by exactly one tile.
All inputs are finite; a program needn't handle non-finite values.
Results may differ from a plain program's by a relative error of at most 0.0062.
Values may be sent and summed in bfloat16 or wider, within the bound.
A program may use at most 128 MiB of HBM per device.

v0:
```python
import jax
import jax.numpy as jnp
from jax import lax
from jax.sharding import PartitionSpec as P


def tile_products(sources, tile_block, row_ids, src_ids, nblocks):
    chosen = jnp.take(sources, src_ids, axis=1)
    products = jnp.einsum("ktc,trc->ktr", chosen, tile_block, preferred_element_type=jnp.float32)
    onehot = (row_ids[None, :] == jnp.arange(nblocks, dtype=jnp.int32)[:, None]).astype(jnp.float32)
    summed = jnp.einsum("bt,ktr->kbr", onehot, products, precision=lax.Precision.HIGHEST)
    return summed.reshape(summed.shape[0], -1)


def apply_operator(vectors, tile_vals, tile_row, tile_src, send_list):
    columns, length = vectors.shape
    tile_side = tile_vals.shape[1]
    nblocks = length // tile_side
    blocked = vectors.reshape(columns, nblocks, tile_side)
    outgoing = jnp.take(blocked, send_list.reshape(-1), axis=1)
    incoming = lax.all_to_all(outgoing, "rows", split_axis=1, concat_axis=1, tiled=True)
    row_ids = tile_row.reshape(-1)
    src_ids = tile_src.reshape(-1)
    sources = jnp.concatenate([blocked, incoming], axis=1)
    return tile_products(sources, tile_vals, row_ids, src_ids, nblocks)


def contract_nodes(left_side, right_side):
    return lax.dot_general(
        left_side, right_side, (((1,), (1,)), ((), ())), preferred_element_type=jnp.float32
    )


def body(vectors, tile_vals, tile_row, tile_src, send_list, ritz_matrix):
    first_pass = apply_operator(vectors, tile_vals, tile_row, tile_src, send_list).astype(
        jnp.bfloat16
    )
    second = apply_operator(first_pass, tile_vals, tile_row, tile_src, send_list)
    filtered = (2.0 * second - vectors.astype(jnp.float32)).astype(jnp.bfloat16)
    total_nodes = vectors.shape[1] * lax.axis_size("rows")
    operated = apply_operator(filtered, tile_vals, tile_row, tile_src, send_list).astype(
        jnp.bfloat16
    )
    portion = lax.all_gather(filtered, "cols", axis=0, tiled=True)
    gram_piece = contract_nodes(filtered, portion)
    proj_piece = contract_nodes(operated, portion)
    turned = lax.dot_general(
        ritz_matrix, portion, (((0,), (0,)), ((), ())), preferred_element_type=jnp.float32
    )
    gram_total, proj_total = lax.psum((gram_piece, proj_piece), "rows")
    gram_matrix = gram_total / total_nodes
    projected = proj_total / total_nodes
    rotated = turned.astype(jnp.bfloat16)
    return (rotated, gram_matrix, projected)


def solution(mesh):
    return jax.shard_map(
        body,
        mesh=mesh,
        in_specs=(
            P("cols", "rows"),
            P("rows", None, None),
            P("rows", None),
            P("rows", None),
            P("rows", None),
            P(None, "cols"),
        ),
        out_specs=(P("cols", "rows"), P("cols", None), P("cols", None)),
        check_vma=False,
    )
```

profile of v0, /device:TPU:1, one launch (start us, length us, event | category | flops | bytes accessed | tf_op | source)
XLA Modules:
  0.0 433.8 jit_solution(941377875002541692)
XLA Ops:
  7.2 0.8 copy.13
  8.1 1.1 copy.44
  9.2 0.6 gather_fusion
  9.9 1.2 select_bitcast_fusion.2
  11.1 13.1 %all-to-all-start = ((bf16[16,128,256]{2,0,1:T(8,128)(2,1)}), bf16[16,128,256]{2,0,1:T(8,128)(2,1)S(1)}, u32[]{:S(2)}, u32[]{:S(2)}) async-start(bf16[16,128,256]{2,0,1:T(8,128)(2,1)} %select_bitcast_fusion.2), calls=%async_computation | async-start | bytes 2097152 | tf_op jit(solution)/shard_map/all_to_all | solution.py:21
  24.2 27.9 %all-to-all-done = bf16[16,128,256]{2,0,1:T(8,128)(2,1)S(1)} async-done(((bf16[16,128,256]{2,0,1:T(8,128)(2,1)}), bf16[16,128,256]{2,0,1:T(8,128)(2,1)S(1)}, u32[]{:S(2)}, u32[]{:S(2)}) %all-to-all-start) | async-done | bytes 1048608 | tf_op jit(solution)/shard_map/all_to_all | solution.py:21
  52.3 2.0 gather_fusion.1
  54.3 12.0 %convolution_bitcast_fusion.2 = f32[16,192,256]{2,0,1:T(8,128)S(1)} fusion(bf16[192,256,256]{2,1,0:T(8,128)(2,1)} %param.11, bf16[192,16,256]{2,1,0:T(8,128)(2,1)} %gather_fusion.1, pred[192]{0:T(512)(128)(4,1)S(1)} %compare_and_fusion), kind=kOutput, calls=%fused_computation.16 | convolution fusion | flops 403439616 | bytes 29884608 | tf_op jit(solution)/shard_map/ktc,trc->ktr/dot_general | solution.py:9
  66.4 3.2 fusion.25
  70.7 34.2 %all_to_all.15 = bf16[16,128,256]{2,0,1:T(8,128)(2,1)S(1)} all-to-all(bf16[16,128,256]{2,0,1:T(8,128)(2,1)S(1)} %select_bitcast_fusion.1), channel_id=1, replica_groups=mesh['rows'=64,'cols'=4] {'rows'}, dimensions={1} | all-to-all | bytes 2097152 | tf_op jit(solution)/shard_map/all_to_all | solution.py:21
  105.1 2.0 gather_fusion.3
  107.1 12.0 %convolution_bitcast_fusion.1 = f32[16,192,256]{2,0,1:T(8,128)S(1)} fusion(bf16[192,256,256]{2,1,0:T(8,128)(2,1)} %param.11, bf16[192,16,256]{2,1,0:T(8,128)(2,1)} %gather_fusion.3, pred[192]{0:T(512)(128)(4,1)S(1)} %compare_and_fusion), kind=kOutput, calls=%fused_computation.15 | convolution fusion | flops 403439616 | bytes 29884608 | tf_op jit(solution)/shard_map/ktc,trc->ktr/dot_general | solution.py:9
  119.2 3.2 fusion.16
  124.3 1.2 select_bitcast_fusion
  125.5 6.6 %all-to-all-start.2 = ((bf16[16,128,256]{2,0,1:T(8,128)(2,1)}), bf16[16,128,256]{2,0,1:T(8,128)(2,1)}, u32[]{:S(2)}, u32[]{:S(2)}) async-start(bf16[16,128,256]{2,0,1:T(8,128)(2,1)} %select_bitcast_fusion), calls=%async_computation.2 | async-start | bytes 2097152 | tf_op jit(solution)/shard_map/all_to_all | solution.py:21
  132.9 27.2 %all-to-all-done.2 = bf16[16,128,256]{2,0,1:T(8,128)(2,1)} async-done(((bf16[16,128,256]{2,0,1:T(8,128)(2,1)}), bf16[16,128,256]{2,0,1:T(8,128)(2,1)}, u32[]{:S(2)}, u32[]{:S(2)}) %all-to-all-start.2) | async-done | bytes 1048608 | tf_op jit(solution)/shard_map/all_to_all | solution.py:21
  160.0 1.4 pad_maximum_fusion.2
  161.4 2.0 gather_fusion.5
  163.5 12.1 %convolution_bitcast_fusion = f32[16,192,256]{2,0,1:T(8,128)S(1)} fusion(bf16[192,256,256]{2,1,0:T(8,128)(2,1)} %param.11, bf16[192,16,256]{2,1,0:T(8,128)(2,1)} %gather_fusion.5, pred[192]{0:T(512)(128)(4,1)S(1)} %compare_and_fusion), kind=kOutput, calls=%fused_computation.14 | convolution fusion | flops 403439616 | bytes 29884608 | tf_op jit(solution)/shard_map/ktc,trc->ktr/dot_general | solution.py:9
  175.5 3.2 fusion.22
  179.0 2.5 fusion.41
  181.6 0.7 fusion.42
  182.2 243.0 %all-reduce = (f32[16,64]{1,0:T(8,128)S(1)}, f32[16,64]{1,0:T(8,128)S(1)}) all-reduce(f32[16,64]{1,0:T(8,128)S(1)} %fusion.41, f32[16,64]{1,0:T(8,128)S(1)} %fusion.42), channel_id=1, replica_groups=mesh['rows'=64,'cols'=4] {'rows'}, use_global_device_ids=true, to_apply=%region_0.3 | all-reduce | flops 2048 | bytes 16384 | tf_op jit(solution)/shard_map/psum | solution.py:50
  425.8 1.2 fusion
  (33 shorter events, 5.2 us)
Async XLA Ops:
  7.2 418.6 %copy-start = (bf16[64,16]{0,1:T(8,128)(2,1)S(1)}, bf16[64,16]{0,1:T(8,128)(2,1)}, u32[]{:S(2)}) copy-start(bf16[64,16]{0,1:T(8,128)(2,1)} %param.15) | copy-start | bytes 6148
  11.1 13.1 %copy-start.5 = (s32[1,192]{1,0:T(1,128)S(1)}, s32[1,192]{1,0:T(1,128)}, u32[]{:S(2)}) copy-start(s32[1,192]{1,0:T(1,128)} %param.13) | copy-start | bytes 2308
  11.1 41.1 %all-to-all-start = ((bf16[16,128,256]{2,0,1:T(8,128)(2,1)}), bf16[16,128,256]{2,0,1:T(8,128)(2,1)S(1)}, u32[]{:S(2)}, u32[]{:S(2)}) async-start(bf16[16,128,256]{2,0,1:T(8,128)(2,1)} %select_bitcast_fusion.2), calls=%async_computation | async-start | bytes 2097152 | tf_op jit(solution)/shard_map/all_to_all | solution.py:21
  54.3 12.1 %copy-start.4 = (s32[1,192]{1,0:T(1,128)S(1)}, s32[1,192]{1,0:T(1,128)}, u32[]{:S(2)}) copy-start(s32[1,192]{1,0:T(1,128)} %param.12) | copy-start | bytes 2308
  122.3 1.0 copy-start.3
  123.5 0.8 copy-start.2
  125.5 34.6 %all-to-all-start.2 = ((bf16[16,128,256]{2,0,1:T(8,128)(2,1)}), bf16[16,128,256]{2,0,1:T(8,128)(2,1)}, u32[]{:S(2)}, u32[]{:S(2)}) async-start(bf16[16,128,256]{2,0,1:T(8,128)(2,1)} %select_bitcast_fusion), calls=%async_computation.2 | async-start | bytes 2097152 | tf_op jit(solution)/shard_map/all_to_all | solution.py:21
  132.1 46.9 %all-gather.2.cloned.1.call-start = ((), (), s32[]{:S(2)}) async-start(), calls=%async_computation.3 | async-start | bytes 2621440 | tf_op jit(solution)/shard_map/all_gather | solution.py:44
  179.0 2.6 copy-start.1
Sparse Core Ops, SparseCore 0:
  135.4 34.5 all-gather.1
where the time goes:
time: 438 us; the launch traced here: 434 us
  blocking collectives  277 us (63%)
  waiting for transfers between devices  55.6 us (13%)
  matrix products  50 us (11%)
  starting transfers between devices  20 us (5%)
  between operations  14.2 us (3%)
  local copies, waits for them, and re-layouts  11.8 us (3%)
  other arithmetic  4.97 us (1%)
    psum x1, blocking collectives, body(): gram_total, proj_total = lax.psum((gram_piece, proj_piece), 'rows')  243 us
    all_to_all x2, waiting for transfers between devices, apply_operator(): lax.all_to_all(outgoing, 'rows', split_axis=1, concat_axis=1, tiled=True)  55.1 us
    dot_general x3, matrix products, tile_products(): jnp.einsum('ktc,trc->ktr', chosen, tile_block, preferred_element_type=jnp...  36.1 us
    all_to_all x1, blocking collectives, apply_operator(): lax.all_to_all(outgoing, 'rows', split_axis=1, concat_axis=1, tiled=True)  34.2 us
    all_to_all x2, starting transfers between devices, apply_operator(): lax.all_to_all(outgoing, 'rows', split_axis=1, concat_axis=1, tiled=True)  19.8 us
    dot_general x3, matrix products, tile_products(): jnp.einsum('bt,ktr->kbr', onehot, products, precision=lax.Precision.HIGHEST)  9.49 us
  transfers between devices with their start and end apart: 3, of which 2 were waited for; matrix products, arithmetic and copies ran while one was open for 4% of the time, Pallas kernels for 0%

commit v1 on v0

v1 whole, which is shorter than its diff:
```python
import functools

import jax
import jax.numpy as jnp
from jax import lax
from jax.experimental import pallas as pl
from jax.experimental.pallas import tpu as pltpu
from jax.sharding import PartitionSpec as P

MESH = pl.DeviceIdType.MESH
F32, BF16 = jnp.float32, jnp.bfloat16
X, C = 4, 2
HV = 8
CH = 4
DIMS = dict(x=X, c=C)


def unrolled(count, unroll, step):
    assert count % unroll == 0

    def body(i, carry):
        for u in range(unroll):
            step(i * unroll + u)
        return carry

    lax.fori_loop(0, count // unroll, body, 0)


def kernel(
    n, ny, nb, nt, total_nodes,
    inv_ref, slot_ref, same_ref, last_ref, send_ref, vec_ref, ritz_ref, tiles_hbm,
    rot_ref, gram_ref, proj_ref,
    tiles, cur, outb, land, prods, accs, opb, full, red1, red2,
    tile_sem, ssem, rsem, ysend, yrecv, qsend, qrecv,
):
    Z = n // (X * C)
    me, cy = lax.axis_index("rows"), lax.axis_index("cols")
    z, x, c = lax.div(me, X * C), lax.rem(lax.div(me, C), X), lax.rem(me, C)
    ntc = nt // tile_sem.shape[0]
    per = n // CH

    def split(k):
        return lax.rem(k, Z), lax.rem(lax.div(k, Z), X), lax.div(k, Z * X)

    def target(k):
        dz, dx, dc = split(k)
        return (lax.rem(z + dz, Z) * X + lax.rem(x + dx, X)) * C + lax.rem(c + dc, C)

    def origin(k):
        dz, dx, dc = split(k)
        return (lax.rem(z - dz + Z, Z) * X + lax.rem(x - dx + X, X)) * C + lax.rem(c - dc + C, C)

    loads = [
        pltpu.make_async_copy(
            tiles_hbm.at[pl.ds(i * ntc, ntc)], tiles.at[pl.ds(i * ntc, ntc)], tile_sem.at[i]
        )
        for i in range(tile_sem.shape[0])
    ]
    for load in loads:
        load.start()

    barrier = pltpu.get_barrier_semaphore()

    def greet(k, carry):
        pl.semaphore_signal(barrier, inc=1, device_id={"rows": target(k)}, device_id_type=MESH)
        return carry

    lax.fori_loop(1, n, greet, 0)
    for d in range(1, ny):
        pl.semaphore_signal(
            barrier, inc=1, device_id={"cols": lax.rem(cy + d, ny)}, device_id_type=MESH
        )

    def unpack(r):
        both = vec_ref[:, pl.ds(pl.multiple_of(r * 256, 256), 256)].astype(F32)
        cur[0, 0, r] = both[:HV]
        cur[0, 1, r] = both[HV:]

    unrolled(nb, 8, unpack)

    def chosen(side, h, dest):
        return jnp.concatenate(
            [cur[side, h, send_ref[dest, 0]], cur[side, h, send_ref[dest, 1]]], axis=0
        ).astype(BF16)

    def pack(p, h):
        side = p % 2
        land[p, h, 0] = chosen(side, h, me)

        def step(k):
            outb[p, h, k] = chosen(side, h, target(k))

        unrolled(n, 8, step)

    def message(p, h, k, dest):
        return pltpu.make_async_remote_copy(
            src_ref=outb.at[p, h, k], dst_ref=land.at[p, h, k],
            send_sem=ssem.at[p, h], recv_sem=rsem.at[p, h, lax.div(k, per)],
            device_id={"rows": dest}, device_id_type=MESH,
        )

    def send(p, h):
        def step(k, carry):
            message(p, h, k, target(k)).start()
            return carry

        lax.fori_loop(1, n, step, 0)

    def arrived(p, h, g):
        low = max(1, g * per)
        count = (g + 1) * per - low
        pltpu.make_async_remote_copy(
            src_ref=outb.at[p, h, pl.ds(low, count)], dst_ref=land.at[p, h, pl.ds(low, count)],
            send_sem=ssem.at[p, h], recv_sem=rsem.at[p, h, g],
            device_id={"rows": target(1)}, device_id_type=MESH,
        ).wait_recv()

    def sent(p, h):
        pltpu.make_async_remote_copy(
            src_ref=outb.at[p, h, pl.ds(1, n - 1)], dst_ref=land.at[p, h, pl.ds(1, n - 1)],
            send_sem=ssem.at[p, h], recv_sem=rsem.at[p, h, 0],
            device_id={"rows": target(1)}, device_id_type=MESH,
        ).wait_send()

    def product(rows, tile):
        return lax.dot_general(
            rows, tiles[tile], (((1,), (1,)), ((), ())), preferred_element_type=F32
        )

    def own_products(p, h):
        def step(s):
            prods[h, s] = product(cur[p % 2, h, s].astype(BF16), inv_ref[s])

        unrolled(nb, 8, step)

    def received_products(p, h):
        for g in range(CH):
            arrived(p, h, g)

            def step(i):
                k = g * per + i
                s = nb + 2 * origin(k)
                block = land[p, h, k]
                prods[h, s] = product(block, inv_ref[s])[:HV]
                prods[h, s + 1] = product(block, inv_ref[s + 1])[HV:]

            unrolled(per, 4, step)

    def combine(h, emit):
        def add(i, total):
            for u in range(8):
                k = i * 8 + u
                total = total * same_ref[k] + prods[h, slot_ref[k]]
                accs[k] = total
            return total

        lax.fori_loop(0, nt // 8, add, jnp.zeros((HV, 256), F32))

        def pair(i):
            emit(i, accs[last_ref[2 * i]], accs[last_ref[2 * i + 1]])

        unrolled(nb // 2, 4, pair)

    def across(h, d):
        return pltpu.make_async_remote_copy(
            src_ref=full.at[cy, h], dst_ref=full.at[cy, h],
            send_sem=ysend.at[h, d - 1], recv_sem=yrecv.at[h, d - 1],
            device_id={"cols": lax.rem(cy + d, ny)}, device_id_type=MESH,
        )

    def across_arrival(h, d):
        slot = lax.rem(cy - d + ny, ny)
        return pltpu.make_async_remote_copy(
            src_ref=full.at[slot, h], dst_ref=full.at[slot, h],
            send_sem=ysend.at[h, d - 1], recv_sem=yrecv.at[h, d - 1],
            device_id={"cols": lax.rem(cy + d, ny)}, device_id_type=MESH,
        )

    accs[nt] = jnp.zeros((HV, 256), F32)
    pack(0, 0)
    pl.semaphore_wait(barrier, n - 1 + ny - 1)
    send(0, 0)
    pack(0, 1)
    send(0, 1)
    for load in loads:
        load.wait()

    def first(h):
        def emit(i, a, b):
            cur[1, h, 2 * i] = a.astype(BF16).astype(F32)
            cur[1, h, 2 * i + 1] = b.astype(BF16).astype(F32)

        return emit

    def second(h):
        def emit(i, a, b):
            old = vec_ref[:, pl.ds(pl.multiple_of(i * 512, 512), 512)].astype(F32)
            old = old[h * HV : (h + 1) * HV]
            both = jnp.concatenate([2.0 * a - old[:, :256], 2.0 * b - old[:, 256:]], axis=0)
            both = both.astype(BF16)
            full[cy, h, i] = both
            both = both.astype(F32)
            cur[0, h, 2 * i] = both[:HV]
            cur[0, h, 2 * i + 1] = both[HV:]

        return emit

    def third(h):
        def emit(i, a, b):
            opb[h, i] = jnp.concatenate([a, b], axis=0).astype(BF16)

        return emit

    for p, maker in ((0, first), (1, second)):
        for h in (0, 1):
            own_products(p, h)
            received_products(p, h)
            combine(h, maker(h))
            pack(p + 1, h)
            send(p + 1, h)
            if p == 1:
                for d in range(1, ny):
                    across(h, d).start()

    own_products(2, 0)
    own_products(2, 1)
    received_products(2, 0)
    combine(0, third(0))

    wide = ny * 2 * 2 * HV
    narrow = ny * 2 * HV
    column = lax.broadcasted_iota(jnp.int32, (narrow, wide), 1)
    vector = lax.broadcasted_iota(jnp.int32, (narrow, wide), 0)
    matches = lax.div(column, 32) * 16 + lax.rem(lax.div(column, 16), 2) * 8 + lax.rem(column, 8) == vector
    parity = lax.rem(lax.div(column, 8), 2)
    ritz = ritz_ref[...]
    turns = [
        lax.dot_general(
            ritz, jnp.where(matches & (parity == q), 1.0, 0.0).astype(BF16),
            (((0,), (0,)), ((), ())), preferred_element_type=F32,
        )
        for q in (0, 1)
    ]
    turn = jnp.concatenate(turns, axis=0).astype(BF16)

    for h in (0, 1):
        for d in range(1, ny):
            across_arrival(h, d).wait_recv()

    def weights(i):
        return full[:, :, i].reshape(wide, 256)

    def contract(rows, i):
        return lax.dot_general(
            rows, weights(i), (((1,), (1,)), ((), ())), preferred_element_type=F32
        )

    def beside(j, total):
        for u in range(4):
            i = j * 4 + u
            both = jnp.concatenate([full[cy, 0, i], full[cy, 1, i], opb[0, i]], axis=0)
            total = total + contract(both, i)
            turned = jnp.dot(turn, weights(i), preferred_element_type=F32).astype(BF16)
            at = pl.multiple_of(i * 512, 512)
            rot_ref[:, pl.ds(at, 256)] = turned[: 2 * HV]
            rot_ref[:, pl.ds(at + 256, 256)] = turned[2 * HV :]
        return total

    early = lax.fori_loop(0, nb // 8, beside, jnp.zeros((6 * HV, wide), F32))

    received_products(2, 1)
    combine(1, third(1))

    def ending(j, total):
        for u in range(4):
            i = j * 4 + u
            total = total + contract(opb[1, i], i)
        return total

    late = lax.fori_loop(0, nb // 8, ending, jnp.zeros((2 * HV, wide), F32))
    sums = jnp.concatenate([early, late], axis=0).reshape(4, 2, HV, wide)
    odd = lax.rem(lax.div(lax.broadcasted_iota(jnp.int32, (4, HV, wide), 2), 8), 2) == 1
    sums = jnp.where(odd, sums[:, 1], sums[:, 0]).reshape(4 * HV, wide)
    picked = lax.dot_general(
        sums, jnp.where(matches, 1.0, 0.0).astype(F32), (((1,), (1,)), ((), ())),
        precision=lax.Precision.HIGHEST, preferred_element_type=F32,
    )
    mine = jnp.concatenate([picked[: 2 * HV], picked[2 * HV :]], axis=1)

    def reduce(stage, red, mine, position, count, to):
        red[position] = mine

        def copies(d, slot):
            return pltpu.make_async_remote_copy(
                src_ref=red.at[slot], dst_ref=red.at[slot],
                send_sem=qsend.at[stage, d - 1], recv_sem=qrecv.at[stage, d - 1],
                device_id={"rows": to(d)}, device_id_type=MESH,
            )

        for d in range(1, count):
            copies(d, position).start()
        for d in range(1, count):
            copies(d, lax.rem(position - d + count, count)).wait_recv()
        total = red[0]
        for d in range(1, count):
            total = total + red[d]
        for d in range(1, count):
            copies(d, position).wait_send()
        return total

    plane = X * C
    spot = lax.rem(me, plane)
    mine = reduce(0, red1, mine, spot, plane, lambda d: z * plane + lax.rem(spot + d, plane))
    mine = reduce(1, red2, mine, z, Z, lambda d: lax.rem(z + d, Z) * plane + spot)
    mine = mine * (1.0 / total_nodes)
    gram_ref[...] = mine[:, :narrow]
    proj_ref[...] = mine[:, narrow:]
    for p in range(3):
        for h in (0, 1):
            sent(p, h)
    for h in (0, 1):
        for d in range(1, ny):
            across(h, d).wait_send()


def orders(tile_row, tile_src, nb):
    row, src = tile_row.reshape(-1), tile_src.reshape(-1)
    nt = row.shape[0]
    at = jnp.arange(nt, dtype=jnp.int32)
    inverse = jnp.sum(jnp.where(src[:, None] == at[None, :], at[:, None], 0), axis=0)
    key = row * nt + at
    rank = jnp.sum((key[None, :] < key[:, None]).astype(jnp.int32), axis=1)
    placed = rank[:, None] == at[None, :]
    slot = jnp.sum(jnp.where(placed, src[:, None], 0), axis=0)
    rows = jnp.sum(jnp.where(placed, row[:, None], 0), axis=0)
    before = jnp.sum(jnp.where(rank[:, None] + 1 == at[None, :], row[:, None] + 1, 0), axis=0) - 1
    same = (rows == before).astype(F32)
    blocks = jnp.arange(nb, dtype=jnp.int32)
    upto = jnp.sum((row[:, None] <= blocks[None, :]).astype(jnp.int32), axis=0)
    under = jnp.sum((row[:, None] < blocks[None, :]).astype(jnp.int32), axis=0)
    last = jnp.where(upto > under, upto - 1, nt)
    return inverse, slot, same, last


def solution(mesh):
    n, ny = mesh.shape["rows"], mesh.shape["cols"]

    def body(vectors, tile_vals, tile_row, tile_src, send_list, ritz):
        nt = tile_vals.shape[0]
        nb = vectors.shape[1] // 256
        k = ritz.shape[0]
        inverse, slot, same, last = orders(tile_row, tile_src, nb)
        smem = pl.BlockSpec(memory_space=pltpu.SMEM)
        vmem = pl.BlockSpec(memory_space=pltpu.VMEM)
        dma = pltpu.SemaphoreType.DMA
        return pl.pallas_call(
            functools.partial(kernel, n, ny, nb, nt, vectors.shape[1] * n),
            out_shape=(
                jax.ShapeDtypeStruct(vectors.shape, BF16),
                jax.ShapeDtypeStruct((2 * HV, k), F32),
                jax.ShapeDtypeStruct((2 * HV, k), F32),
            ),
            in_specs=[smem] * 5 + [vmem] * 2 + [pl.BlockSpec(memory_space=pl.ANY)],
            out_specs=(vmem, vmem, vmem),
            scratch_shapes=[
                pltpu.VMEM((nt, 256, 256), BF16),
                pltpu.VMEM((2, 2, nb, HV, 256), F32),
                pltpu.VMEM((3, 2, n, 2 * HV, 256), BF16),
                pltpu.VMEM((3, 2, n, 2 * HV, 256), BF16),
                pltpu.VMEM((2, nt, HV, 256), F32),
                pltpu.VMEM((nt + 1, HV, 256), F32),
                pltpu.VMEM((2, nb // 2, 2 * HV, 256), BF16),
                pltpu.VMEM((ny, 2, nb // 2, 2 * HV, 256), BF16),
                pltpu.VMEM((X * C, 2 * HV, 2 * k), F32),
                pltpu.VMEM((n // (X * C), 2 * HV, 2 * k), F32),
                dma((8,)),
                dma((3, 2)),
                dma((3, 2, CH)),
                dma((2, ny - 1)),
                dma((2, ny - 1)),
                dma((2, 7)),
                dma((2, 7)),
            ],
            compiler_params=pltpu.CompilerParams(
                collective_id=0, has_side_effects=True, vmem_limit_bytes=56 << 20
            ),
        )(inverse, slot, same, last, send_list, vectors, ritz, tile_vals)

    return jax.shard_map(
        body,
        mesh=mesh,
        in_specs=(
            P("cols", "rows"),
            P("rows", None, None),
            P("rows", None),
            P("rows", None),
            P("rows", None),
            P(None, "cols"),
        ),
        out_specs=(P("cols", "rows"), P("cols", None), P("cols", None)),
        check_vma=False,
    )
```

time: 438 us -> 119 us (0.27)
  blocking collectives: 277 us -> 0 us
  Pallas kernels: 0 us -> 106 us
  waiting for transfers between devices: 55.6 us -> 0 us
  matrix products: 50 us -> 0 us
  starting transfers between devices: 20 us -> 0 us
  between operations: 14.2 us -> 0.66 us
  local copies, waits for them, and re-layouts: 11.8 us -> 7.21 us
    psum x1 -> x0, blocking collectives: 243 us -> none  [body(): gram_total, proj_total = lax.psum((gram_piece, proj_piece), 'rows')]
    pallas_call x0 -> x1, Pallas kernels: none -> 106 us  [body(): pl.pallas_call(functools.partial(kernel, n, ny, nb, nt, vectors.shape[1]...]
    all_to_all x2 -> x0, waiting for transfers between devices: 55.1 us -> none  [apply_operator(): lax.all_to_all(outgoing, 'rows', split_axis=1, concat_axis=1, tiled=True)]
    dot_general x9 -> x0, matrix products: 50 us -> none  [the longest x3 36.1 us: tile_products(): jnp.einsum('ktc,trc->ktr', chosen, tile_block, preferred_element_type=jnp...]
    all_to_all x1 -> x0, blocking collectives: 34.2 us -> none  [apply_operator(): lax.all_to_all(outgoing, 'rows', split_axis=1, concat_axis=1, tiled=True)]
    all_to_all x2 -> x0, starting transfers between devices: 19.8 us -> none  [apply_operator(): lax.all_to_all(outgoing, 'rows', split_axis=1, concat_axis=1, tiled=True)]
    gather x6 -> x0, local copies, waits for them, and re-layouts: 8.04 us -> none  [the longest x3 6.1 us: tile_products(): chosen = jnp.take(sources, src_ids, axis=1)]
    unnamed x15 -> x5, local copies, waits for them, and re-layouts: 2.22 us -> 7.21 us
  transfers between devices with their start and end apart: 3 -> 0, of which waited for: 2 -> 0; matrix products, arithmetic and copies ran while one was open for 4% -> 0% of each run, Pallas kernels for 0% -> 0%
where the time goes in v1:
time: 119 us
  Pallas kernels  106 us (89%)
  local copies, waits for them, and re-layouts  7.21 us (6%)
  other arithmetic  4.89 us (4%)
    pallas_call x1, Pallas kernels, body(): pl.pallas_call(functools.partial(kernel, n, ny, nb, nt, vectors.shape[1]...  106 us
    unnamed x5, local copies, waits for them, and re-layouts  7.21 us

profile of v1, /device:TPU:1, one launch (start us, length us, event | category | flops | bytes accessed | tf_op | source)
XLA Modules:
  0.0 118.5 jit_solution(11792388575970901118)
XLA Ops:
  0.6 0.7 iota_add_fusion.1
  1.3 0.8 convert_reduce_fusion.1
  2.1 0.5 compare_select_fusion.last_ref
  2.6 0.7 broadcast_add_fusion
  3.3 0.2 convert_reduce_fusion
  3.5 1.5 %select_reduce_fusion.1 = (s32[192]{0:T(256)S(1)}, s32[192]{0:T(256)}, s32[192]{0:T(256)}, s32[192]{0:T(256)S(1)}) fusion(s32[192]{0:T(256)} %bitcast.5, s32[192]{0:T(256)S(1)} %convert_reduce_fusion, s32[192]{0:T(256)} %bitcast.7, s32[192]{0:T(256)S(1)} %get-tuple-element.8, s32[192]{0:T(256)S(1)} %broadcast_add_fusion.1), kind=kLoop, calls=%fused_computation.2 | loop fusion | flops 404736 | bytes 6912 | tf_op jit(solution)/shard_map/reduce_sum | solution.py:335
  5.0 0.5 compare_convert_fusion.same_ref
  5.5 1.4 %copy.12.ritz_ref = bf16[64,16]{1,0:T(8,128)(2,1)} copy(bf16[64,16]{0,1:T(8,128)(2,1)} %param.11) | data formatting | bytes 4096 | tf_op args[5]
  6.9 1.4 %copy.11.send_ref = s32[64,2]{1,0:T(8,128)} copy(s32[64,2]{0,1:T(2,128)} %param.10) | data formatting | bytes 1024 | tf_op args[4]
  8.3 105.8 %shard_map.85 = (bf16[16,16384]{1,0:T(8,128)(2,1)}, f32[16,64]{1,0:T(8,128)}, f32[16,64]{1,0:T(8,128)}) custom-call(s32[192]{0:T(256)} %get-tuple-element.7.inv_ref, s32[192]{0:T(256)} %get-tuple-element.6.slot_ref, f32[192]{0:T(256)} %compare_convert_fusion.same_ref, s32[64]{0:T(128)} %compare_select_fusion.last_ref, s32[64,2]{1,0:T(8,128)} %copy.11.send_ref, ...), custom_call_target="tpu_custom_call" | custom-call | tf_op jit(solution)/shard_map/pallas_call | solution.py:356
  114.1 1.9 %copy.16 = bf16[16,16384]{1,0:T(8,128)(2,1)} copy(bf16[16,16384]{1,0:T(8,128)(2,1)} %get-tuple-element.14) | data formatting | bytes 1048576
  116.0 1.3 %copy.17 = f32[16,64]{1,0:T(8,128)} copy(f32[16,64]{1,0:T(8,128)} %get-tuple-element.15) | data formatting | bytes 8192
  117.2 1.3 %copy.18 = f32[16,64]{1,0:T(8,128)} copy(f32[16,64]{1,0:T(8,128)} %get-tuple-element.16) | data formatting | bytes 8192
  (1 shorter events, 0.0 us)

commit v2 on v1

v2 whole, which is shorter than its diff:
```python
import functools

import jax
import jax.numpy as jnp
from jax import lax
from jax.experimental import pallas as pl
from jax.experimental.pallas import tpu as pltpu
from jax.sharding import PartitionSpec as P

MESH = pl.DeviceIdType.MESH
F32, BF16 = jnp.float32, jnp.bfloat16
X, C = 4, 2
HV = 8
CH = 4
DIMS = dict(x=X, c=C)


def unrolled(count, unroll, step):
    assert count % unroll == 0

    def body(i, carry):
        for u in range(unroll):
            step(i * unroll + u)
        return carry

    lax.fori_loop(0, count // unroll, body, 0)


def kernel(
    n, ny, nb, nt, total_nodes,
    row_ref, src_ref, send_ref, ritz_ref, vec_hbm, tiles_hbm,
    rot_ref, sums_ref,
    vec_ref, tiles, cur, outb, land, prods, accs, opb, full, red1, red2,
    index_v, same_v, index_s, same_s,
    vec_sem, index_sem, tile_sem, ssem, rsem, ysend, yrecv, qsend, qrecv,
):
    Z = n // (X * C)
    me, cy = lax.axis_index("rows"), lax.axis_index("cols")
    z, x, c = lax.div(me, X * C), lax.rem(lax.div(me, C), X), lax.rem(me, C)
    ntc = nt // tile_sem.shape[0]
    per = n // CH

    def split(k):
        return lax.rem(k, Z), lax.rem(lax.div(k, Z), X), lax.div(k, Z * X)

    def target(k):
        dz, dx, dc = split(k)
        return (lax.rem(z + dz, Z) * X + lax.rem(x + dx, X)) * C + lax.rem(c + dc, C)

    def origin(k):
        dz, dx, dc = split(k)
        return (lax.rem(z - dz + Z, Z) * X + lax.rem(x - dx + X, X)) * C + lax.rem(c - dc + C, C)

    loads = [
        pltpu.make_async_copy(
            tiles_hbm.at[pl.ds(i * ntc, ntc)], tiles.at[pl.ds(i * ntc, ntc)], tile_sem.at[i]
        )
        for i in range(tile_sem.shape[0])
    ]
    bring = pltpu.make_async_copy(vec_hbm, vec_ref, vec_sem)
    bring.start()
    zs = [lax.rem(z + d, Z) * (X * C) for d in range(Z)]

    barrier = pltpu.get_barrier_semaphore()

    def each_peer(act):
        def plane(g, carry, first=0):
            dx, dc = lax.rem(g, X), lax.div(g, X)
            rest = lax.rem(x + dx, X) * C + lax.rem(c + dc, C)
            for d in range(first, Z):
                act(g * Z + d, zs[d] + rest)
            return carry

        plane(0, 0, 1)
        lax.fori_loop(1, X * C, plane, 0)

    each_peer(
        lambda k, dest: pl.semaphore_signal(
            barrier, inc=1, device_id={"rows": dest}, device_id_type=MESH
        )
    )
    for d in range(1, ny):
        pl.semaphore_signal(
            barrier, inc=1, device_id={"cols": lax.rem(cy + d, ny)}, device_id_type=MESH
        )

    def unpack(r):
        both = vec_ref[:, pl.ds(pl.multiple_of(r * 256, 256), 256)].astype(F32)
        cur[0, 0, r] = both[:HV]
        cur[0, 1, r] = both[HV:]

    bring.wait()
    for load in loads:
        load.start()
    unrolled(nb, 8, unpack)

    def chosen(side, h, dest):
        return jnp.concatenate(
            [cur[side, h, send_ref[0, dest]], cur[side, h, send_ref[1, dest]]], axis=0
        ).astype(BF16)

    def pack(p, h):
        side = p % 2
        land[p, h, 0] = chosen(side, h, me)

        def step(k, dest):
            outb[p, h, k] = chosen(side, h, dest)

        each_peer(step)

    def message(p, h, k, dest):
        return pltpu.make_async_remote_copy(
            src_ref=outb.at[p, h, k], dst_ref=land.at[p, h, k],
            send_sem=ssem.at[p, h], recv_sem=rsem.at[p, h, lax.div(k, per)],
            device_id={"rows": dest}, device_id_type=MESH,
        )

    def send(p, h):
        each_peer(lambda k, dest: message(p, h, k, dest).start())

    def arrived(p, h, g):
        low = max(1, g * per)
        count = (g + 1) * per - low
        pltpu.make_async_remote_copy(
            src_ref=outb.at[p, h, pl.ds(low, count)], dst_ref=land.at[p, h, pl.ds(low, count)],
            send_sem=ssem.at[p, h], recv_sem=rsem.at[p, h, g],
            device_id={"rows": target(1)}, device_id_type=MESH,
        ).wait_recv()

    def sent(p, h):
        pltpu.make_async_remote_copy(
            src_ref=outb.at[p, h, pl.ds(1, n - 1)], dst_ref=land.at[p, h, pl.ds(1, n - 1)],
            send_sem=ssem.at[p, h], recv_sem=rsem.at[p, h, 0],
            device_id={"rows": target(1)}, device_id_type=MESH,
        ).wait_send()

    def product(rows, tile):
        return lax.dot_general(
            rows, tiles[tile], (((1,), (0,)), ((), ())), preferred_element_type=F32
        )

    def own_products(p, h):
        def step(s):
            prods[h, s] = product(cur[p % 2, h, s].astype(BF16), index_s[0, s])

        unrolled(nb, 8, step)

    def received_products(p, h, g):
        arrived(p, h, g)

        def step(i):
            k = g * per + i
            s = nb + 2 * origin(k)
            block = land[p, h, k]
            prods[h, s] = product(block, index_s[0, s])[:HV]
            prods[h, s + 1] = product(block, index_s[0, s + 1])[HV:]

        unrolled(per, 4, step)

    def add(h, first, count):
        def step(i, total):
            for u in range(8):
                k = first + i * 8 + u
                total = total * same_s[0, k] + prods[h, index_s[1, k]]
                accs[k] = total
            return total

        lax.fori_loop(0, count // 8, step, jnp.zeros((HV, 256), F32))

    def apply(p, h):
        for g in range(CH):
            received_products(p, h, g)
            if g == CH // 2 - 1:
                add(h, 0, nb + n)
        add(h, nb + n, n)

    def summed(r):
        return accs[index_s[2, r]] + accs[index_s[2, nb + r]]

    def pairs(emit):
        unrolled(nb // 2, 4, lambda i: emit(i, summed(2 * i), summed(2 * i + 1)))

    def across(h, d):
        return pltpu.make_async_remote_copy(
            src_ref=full.at[cy, h], dst_ref=full.at[cy, h],
            send_sem=ysend.at[h, d - 1], recv_sem=yrecv.at[h, d - 1],
            device_id={"cols": lax.rem(cy + d, ny)}, device_id_type=MESH,
        )

    def across_arrival(h, d):
        slot = lax.rem(cy - d + ny, ny)
        return pltpu.make_async_remote_copy(
            src_ref=full.at[slot, h], dst_ref=full.at[slot, h],
            send_sem=ysend.at[h, d - 1], recv_sem=yrecv.at[h, d - 1],
            device_id={"cols": lax.rem(cy + d, ny)}, device_id_type=MESH,
        )

    accs[nt] = jnp.zeros((HV, 256), F32)
    pack(0, 0)
    pl.semaphore_wait(barrier, n - 1 + ny - 1)
    send(0, 0)
    pack(0, 1)
    send(0, 1)

    side = (nt, nt)
    down = lax.broadcasted_iota(jnp.int32, side, 0)
    along = lax.broadcasted_iota(jnp.int32, side, 1)

    def upright(line):
        spread = jnp.where(down == along, jnp.broadcast_to(line, side).astype(F32), 0.0)
        return jnp.sum(spread, axis=1, keepdims=True).astype(jnp.int32)

    def gather(where, value):
        return jnp.sum(jnp.where(where, value, 0), axis=0, keepdims=True)

    src = src_ref[...]
    late = (src >= nb) & (lax.rem(lax.div(src - nb, 2), C) != c)
    row = row_ref[...] + jnp.where(late, nb, 0)
    row_c, src_c = upright(row), upright(src)
    key = row * nt + lax.broadcasted_iota(jnp.int32, (1, nt), 1)
    key_c = row_c * nt + lax.broadcasted_iota(jnp.int32, (nt, 1), 0)
    rank_c = jnp.sum(
        jnp.where(key < key_c, 1.0, 0.0).astype(F32), axis=1, keepdims=True
    ).astype(jnp.int32)
    placed = rank_c == along
    index_v[0:1, :nt] = gather(src_c == along, down)
    index_v[1:2, :nt] = gather(placed, src_c)
    upto = gather(row_c <= along, 1)
    under = gather(row_c < along, 1)
    index_v[2:3, :nt] = jnp.where(upto > under, upto - 1, nt)
    same_v[0:1, :nt] = jnp.where(
        gather(placed, row_c) + 1 == gather(rank_c + 1 == along, row_c + 1), 1.0, 0.0
    )
    moves = [
        pltpu.make_async_copy(index_v, index_s, index_sem.at[0]),
        pltpu.make_async_copy(same_v, same_s, index_sem.at[1]),
    ]
    for move in moves:
        move.start()
    for i, load in enumerate(loads):
        load.wait()

        def flip(j, i=i):
            t = i * ntc + j
            tiles[t] = tiles[t].T

        unrolled(ntc, 4, flip)
    for move in moves:
        move.wait()
    own_products(0, 0)
    own_products(0, 1)

    def first(h):
        def emit(i, a, b):
            cur[1, h, 2 * i] = a.astype(BF16).astype(F32)
            cur[1, h, 2 * i + 1] = b.astype(BF16).astype(F32)

        return emit

    def second(h):
        def emit(i, a, b):
            old = vec_ref[:, pl.ds(pl.multiple_of(i * 512, 512), 512)].astype(F32)
            old = old[h * HV : (h + 1) * HV]
            both = jnp.concatenate([2.0 * a - old[:, :256], 2.0 * b - old[:, 256:]], axis=0)
            both = both.astype(BF16)
            full[cy, h, i] = both
            both = both.astype(F32)
            cur[0, h, 2 * i] = both[:HV]
            cur[0, h, 2 * i + 1] = both[HV:]

        return emit

    def third(i, a, b):
        opb[i] = jnp.concatenate([a, b], axis=0).astype(BF16)

    for p, maker in ((0, first), (1, second)):
        for h in (0, 1):
            apply(p, h)
            pairs(maker(h))
            pack(p + 1, h)
            send(p + 1, h)
            if p == 1:
                for d in range(1, ny):
                    across(h, d).start()
            own_products(p + 1, h)

    apply(2, 0)
    pairs(third)

    wide = ny * 2 * 2 * HV
    narrow = ny * 2 * HV
    column = lax.broadcasted_iota(jnp.int32, (narrow, wide), 1)
    vector = lax.broadcasted_iota(jnp.int32, (narrow, wide), 0)
    matches = lax.div(column, 32) * 16 + lax.rem(lax.div(column, 16), 2) * 8 + lax.rem(column, 8) == vector
    parity = lax.rem(lax.div(column, 8), 2)
    turns = [
        lax.dot_general(
            ritz_ref[...], jnp.where(matches & (parity == q), 1.0, 0.0).astype(BF16),
            (((1,), (0,)), ((), ())), preferred_element_type=F32,
        )
        for q in (0, 1)
    ]
    turn = jnp.concatenate(turns, axis=0).astype(BF16)

    apply(2, 1)

    for h in (0, 1):
        for d in range(1, ny):
            across_arrival(h, d).wait_recv()

    def weights(i):
        return full[:, :, i].reshape(wide, 256)

    def contract(j, total):
        for u in range(4):
            i = j * 4 + u
            rest = jnp.concatenate([summed(2 * i), summed(2 * i + 1)], axis=0).astype(BF16)
            rows = jnp.concatenate([full[cy, 0, i], full[cy, 1, i], opb[i], rest], axis=0)
            total = total + lax.dot_general(
                rows, weights(i), (((1,), (1,)), ((), ())), preferred_element_type=F32
            )
        return total

    sums = lax.fori_loop(0, nb // 8, contract, jnp.zeros((8 * HV, wide), F32))

    def rotate():
        def step(i):
            turned = jnp.dot(turn, weights(i), preferred_element_type=F32).astype(BF16)
            at = pl.multiple_of(i * 512, 512)
            rot_ref[:, pl.ds(at, 256)] = turned[: 2 * HV]
            rot_ref[:, pl.ds(at + 256, 256)] = turned[2 * HV :]

        unrolled(nb // 2, 4, step)

    sums = sums.reshape(4, 2, HV, wide)
    odd = lax.rem(lax.div(lax.broadcasted_iota(jnp.int32, (4, HV, wide), 2), 8), 2) == 1
    sums = jnp.where(odd, sums[:, 1], sums[:, 0]).reshape(4 * HV, wide)
    picked = lax.dot_general(
        sums, jnp.where(matches, 1.0, 0.0).astype(F32), (((1,), (1,)), ((), ())),
        precision=lax.Precision.HIGHEST, preferred_element_type=F32,
    )
    mine = jnp.concatenate([picked[: 2 * HV], picked[2 * HV :]], axis=1)

    def reduce(stage, red, mine, position, count, to, meanwhile):
        red[position] = mine

        def copies(d, slot):
            return pltpu.make_async_remote_copy(
                src_ref=red.at[slot], dst_ref=red.at[slot],
                send_sem=qsend.at[stage, d - 1], recv_sem=qrecv.at[stage, d - 1],
                device_id={"rows": to(d)}, device_id_type=MESH,
            )

        for d in range(1, count):
            copies(d, position).start()
        meanwhile()
        for d in range(1, count):
            copies(d, lax.rem(position - d + count, count)).wait_recv()
        total = red[0]
        for d in range(1, count):
            total = total + red[d]
        for d in range(1, count):
            copies(d, position).wait_send()
        return total

    plane = X * C
    spot = lax.rem(me, plane)
    mine = reduce(0, red1, mine, spot, plane, lambda d: z * plane + lax.rem(spot + d, plane), rotate)
    mine = reduce(1, red2, mine, z, Z, lambda d: lax.rem(z + d, Z) * plane + spot, lambda: None)
    mine = mine * (1.0 / total_nodes)
    sums_ref[...] = mine
    for p in range(3):
        for h in (0, 1):
            sent(p, h)
    for h in (0, 1):
        for d in range(1, ny):
            across(h, d).wait_send()


def finish(rot_ref, sums_ref, rotated_hbm, gram_ref, projected_ref, sem):
    rows = rot_ref.shape[1] // sem.shape[0]
    copies = [
        pltpu.make_async_copy(
            rot_ref.at[:, pl.ds(i * rows, rows)], rotated_hbm.at[:, pl.ds(i * rows, rows)], sem.at[i]
        )
        for i in range(sem.shape[0])
    ]
    for copy in copies:
        copy.start()
    k = gram_ref.shape[1]
    gram_ref[...] = sums_ref[:, :k]
    projected_ref[...] = sums_ref[:, k:]
    for copy in copies:
        copy.wait()


def solution(mesh):
    n, ny = mesh.shape["rows"], mesh.shape["cols"]

    def body(vectors, tile_vals, tile_row, tile_src, send_list, ritz):
        nt = tile_vals.shape[0]
        nb = vectors.shape[1] // 256
        k = ritz.shape[0]
        smem = pl.BlockSpec(memory_space=pltpu.SMEM)
        vmem = pl.BlockSpec(memory_space=pltpu.VMEM)
        dma = pltpu.SemaphoreType.DMA
        anywhere = pl.BlockSpec(memory_space=pl.ANY)
        rotated, sums = pl.pallas_call(
            functools.partial(kernel, n, ny, nb, nt, vectors.shape[1] * n),
            out_shape=(
                pltpu.VMEM(vectors.shape, BF16),
                pltpu.VMEM((2 * HV, 2 * k), F32),
            ),
            in_specs=[vmem, vmem, smem, vmem, anywhere, anywhere],
            out_specs=(vmem, vmem),
            scratch_shapes=[
                pltpu.VMEM(vectors.shape, BF16),
                pltpu.VMEM((nt, 256, 256), BF16),
                pltpu.VMEM((2, 2, nb, HV, 256), F32),
                pltpu.VMEM((3, 2, n, 2 * HV, 256), BF16),
                pltpu.VMEM((3, 2, n, 2 * HV, 256), BF16),
                pltpu.VMEM((2, nt, HV, 256), F32),
                pltpu.VMEM((nt + 1, HV, 256), F32),
                pltpu.VMEM((nb // 2, 2 * HV, 256), BF16),
                pltpu.VMEM((ny, 2, nb // 2, 2 * HV, 256), BF16),
                pltpu.VMEM((X * C, 2 * HV, 2 * k), F32),
                pltpu.VMEM((n // (X * C), 2 * HV, 2 * k), F32),
                pltpu.VMEM((8, 256), jnp.int32),
                pltpu.VMEM((8, 256), F32),
                pltpu.SMEM((8, 256), jnp.int32),
                pltpu.SMEM((8, 256), F32),
                dma,
                dma((2,)),
                dma((8,)),
                dma((3, 2)),
                dma((3, 2, CH)),
                dma((2, ny - 1)),
                dma((2, ny - 1)),
                dma((2, 7)),
                dma((2, 7)),
            ],
            compiler_params=pltpu.CompilerParams(
                collective_id=0, has_side_effects=True, vmem_limit_bytes=56 << 20
            ),
        )(tile_row, tile_src, send_list.T, ritz.T, vectors, tile_vals)
        return pl.pallas_call(
            finish,
            out_shape=(
                jax.ShapeDtypeStruct(vectors.shape, BF16),
                jax.ShapeDtypeStruct((2 * HV, k), F32),
                jax.ShapeDtypeStruct((2 * HV, k), F32),
            ),
            in_specs=[vmem, vmem],
            out_specs=(anywhere, vmem, vmem),
            scratch_shapes=[dma((4,))],
            compiler_params=pltpu.CompilerParams(vmem_limit_bytes=4 << 20),
        )(rotated, sums)

    return jax.shard_map(
        body,
        mesh=mesh,
        in_specs=(
            P("cols", "rows"),
            P("rows", None, None),
            P("rows", None),
            P("rows", None),
            P("rows", None),
            P(None, "cols"),
        ),
        out_specs=(P("cols", "rows"), P("cols", None), P("cols", None)),
        check_vma=False,
    )
```

time: 119 us -> 97.4 us (0.82)
  Pallas kernels: 106 us -> 96.6 us
  local copies, waits for them, and re-layouts: 7.21 us -> 0 us
  other arithmetic: 4.89 us -> 0 us
    pallas_call x1, Pallas kernels: 106 us -> 95.2 us  [body(): pl.pallas_call(functools.partial(kernel, n, ny, nb, nt, vectors.shape[1]...]
    unnamed x5 -> x0, local copies, waits for them, and re-layouts: 7.21 us -> none
    reduce_sum x3 -> x0, other arithmetic: 2.45 us -> none  [the longest x1 1.47 us: orders(): rows = jnp.sum(jnp.where(placed, row[:, None], 0), axis=0)]
    pallas_call x0 -> x1, Pallas kernels: none -> 1.42 us  [body(): pl.pallas_call(finish, out_shape=(jax.ShapeDtypeStruct(vectors.shape, BF1...]
    add x3 -> x0, other arithmetic: 1.37 us -> none  [the longest x1 0.69 us: orders(): key = row * nt + at]
where the time goes in v2:
time: 97.4 us; the launch traced here: 97.2 us
  Pallas kernels  96.6 us (99%)
    pallas_call x1, Pallas kernels, body(): pl.pallas_call(functools.partial(kernel, n, ny, nb, nt, vectors.shape[1]...  95.2 us

profile of v2, /device:TPU:1, one launch (start us, length us, event | category | flops | bytes accessed | tf_op | source)
XLA Modules:
  0.0 97.2 jit_solution(5300253528184763751)
XLA Ops:
  0.6 95.2 %shard_map.85 = (bf16[16,16384]{1,0:T(8,128)(2,1)S(1)}, f32[16,128]{1,0:T(8,128)S(1)}) custom-call(s32[1,192]{1,0:T(1,128)} %row_ref.1, s32[1,192]{1,0:T(1,128)} %src_ref.1, s32[2,64]{1,0:T(2,128)} %bitcast.3, bf16[16,64]{1,0:T(8,128)(2,1)} %bitcast.2, bf16[16,16384]{1,0:T(8,128)(2,1)} %vec_hbm.1, bf16[192,256,256]{2,1,0:T(8,128)(2,1)} %tiles_hbm.1), custom_call_target="tpu_custom_call" | custom-call | tf_op jit(solution)/shard_map/pallas_call | solution.py:408
  95.8 1.4 %shard_map.86 = (bf16[16,16384]{1,0:T(8,128)(2,1)}, f32[16,64]{1,0:T(8,128)}, f32[16,64]{1,0:T(8,128)}) custom-call(bf16[16,16384]{1,0:T(8,128)(2,1)S(1)} %get-tuple-element.5.rot_ref, f32[16,128]{1,0:T(8,128)S(1)} %get-tuple-element.6.sums_ref), custom_call_target="tpu_custom_call" | custom-call | tf_op jit(solution)/shard_map/pallas_call | solution.py:446

commit v3 on v2

--- a/solution.py
+++ b/solution.py
@@ -11,8 +11,6 @@
 F32, BF16 = jnp.float32, jnp.bfloat16
 X, C = 4, 2
 HV = 8
-CH = 4
-DIMS = dict(x=X, c=C)
 
 
 def unrolled(count, unroll, step):
@@ -28,28 +26,21 @@
 
 def kernel(
     n, ny, nb, nt, total_nodes,
-    row_ref, src_ref, send_ref, ritz_ref, vec_hbm, tiles_hbm,
+    row_hbm, src_hbm, send_hbm, ritz_hbm, vec_hbm, tiles_hbm,
     rot_ref, sums_ref,
-    vec_ref, tiles, cur, outb, land, prods, accs, opb, full, red1, red2,
+    row_ref, src_ref, send_ref, ritz_ref, vec_ref, tiles, cur, outb, land, prods, accs, opb, full, red1, red2,
     index_v, same_v, index_s, same_s,
-    vec_sem, index_sem, tile_sem, ssem, rsem, ysend, yrecv, qsend, qrecv,
+    small_sem, vec_sem, index_sem, tile_sem, ssem, rsem, ysend, yrecv, qsend, qrecv,
 ):
     Z = n // (X * C)
     me, cy = lax.axis_index("rows"), lax.axis_index("cols")
     z, x, c = lax.div(me, X * C), lax.rem(lax.div(me, C), X), lax.rem(me, C)
     ntc = nt // tile_sem.shape[0]
-    per = n // CH
-
-    def split(k):
-        return lax.rem(k, Z), lax.rem(lax.div(k, Z), X), lax.div(k, Z * X)
-
-    def target(k):
-        dz, dx, dc = split(k)
-        return (lax.rem(z + dz, Z) * X + lax.rem(x + dx, X)) * C + lax.rem(c + dc, C)
-
-    def origin(k):
-        dz, dx, dc = split(k)
-        return (lax.rem(z - dz + Z, Z) * X + lax.rem(x - dx + X, X)) * C + lax.rem(c - dc + C, C)
+    far = sorted(range(Z), key=lambda d: -min(d, Z - d))
+    groups = X * C
+
+    def steps(g):
+        return X - 1 - lax.rem(g, X), C - 1 - lax.div(g, X)
 
     loads = [
         pltpu.make_async_copy(
@@ -59,20 +50,25 @@
     ]
     bring = pltpu.make_async_copy(vec_hbm, vec_ref, vec_sem)
     bring.start()
-    zs = [lax.rem(z + d, Z) * (X * C) for d in range(Z)]
+    pairs_in = ((send_hbm, send_ref), (row_hbm, row_ref), (src_hbm, src_ref), (ritz_hbm, ritz_ref))
+    smalls = [pltpu.make_async_copy(a, b, small_sem.at[i]) for i, (a, b) in enumerate(pairs_in)]
+    for small in smalls:
+        small.start()
+    to_z = [lax.rem(z + d, Z) * groups for d in far]
+    from_z = [lax.rem(z - d + Z, Z) * groups for d in far]
 
     barrier = pltpu.get_barrier_semaphore()
 
     def each_peer(act):
-        def plane(g, carry, first=0):
-            dx, dc = lax.rem(g, X), lax.div(g, X)
+        def plane(g, carry, count=Z):
+            dx, dc = steps(g)
             rest = lax.rem(x + dx, X) * C + lax.rem(c + dc, C)
-            for d in range(first, Z):
-                act(g * Z + d, zs[d] + rest)
+            for j in range(count):
+                act(g * Z + j, to_z[j] + rest)
             return carry
 
-        plane(0, 0, 1)
-        lax.fori_loop(1, X * C, plane, 0)
+        lax.fori_loop(0, groups - 1, plane, 0)
+        plane(groups - 1, 0, Z - 1)
 
     each_peer(
         lambda k, dest: pl.semaphore_signal(
@@ -90,6 +86,8 @@
         cur[0, 1, r] = both[HV:]
 
     bring.wait()
+    for small in smalls:
+        small.wait()
     for load in loads:
         load.start()
     unrolled(nb, 8, unpack)
@@ -101,7 +99,7 @@
 
     def pack(p, h):
         side = p % 2
-        land[p, h, 0] = chosen(side, h, me)
+        land[p, h, n - 1] = chosen(side, h, me)
 
         def step(k, dest):
             outb[p, h, k] = chosen(side, h, dest)
@@ -111,28 +109,20 @@
     def message(p, h, k, dest):
         return pltpu.make_async_remote_copy(
             src_ref=outb.at[p, h, k], dst_ref=land.at[p, h, k],
-            send_sem=ssem.at[p, h], recv_sem=rsem.at[p, h, lax.div(k, per)],
+            send_sem=ssem.at[p, h], recv_sem=rsem.at[p, h, lax.div(k, Z)],
             device_id={"rows": dest}, device_id_type=MESH,
         )
 
     def send(p, h):
         each_peer(lambda k, dest: message(p, h, k, dest).start())
 
-    def arrived(p, h, g):
-        low = max(1, g * per)
-        count = (g + 1) * per - low
-        pltpu.make_async_remote_copy(
-            src_ref=outb.at[p, h, pl.ds(low, count)], dst_ref=land.at[p, h, pl.ds(low, count)],
+    def many(p, h, g, first, count):
+        at = pl.ds(first, count)
+        return pltpu.make_async_remote_copy(
+            src_ref=outb.at[p, h, at], dst_ref=land.at[p, h, at],
             send_sem=ssem.at[p, h], recv_sem=rsem.at[p, h, g],
-            device_id={"rows": target(1)}, device_id_type=MESH,
-        ).wait_recv()
-
-    def sent(p, h):
-        pltpu.make_async_remote_copy(
-            src_ref=outb.at[p, h, pl.ds(1, n - 1)], dst_ref=land.at[p, h, pl.ds(1, n - 1)],
-            send_sem=ssem.at[p, h], recv_sem=rsem.at[p, h, 0],
-            device_id={"rows": target(1)}, device_id_type=MESH,
-        ).wait_send()
+            device_id={"rows": lax.rem(me + 1, n)}, device_id_type=MESH,
+        )
 
     def product(rows, tile):
         return lax.dot_general(
@@ -145,17 +135,15 @@
 
         unrolled(nb, 8, step)
 
-    def received_products(p, h, g):
-        arrived(p, h, g)
-
-        def step(i):
-            k = g * per + i
-            s = nb + 2 * origin(k)
-            block = land[p, h, k]
+    def received_products(p, h, g, count=Z):
+        many(p, h, g, g * Z, count).wait_recv()
+        dx, dc = steps(g)
+        rest = lax.rem(x - dx + X, X) * C + lax.rem(c - dc + C, C)
+        for j in range(Z):
+            s = nb + 2 * (from_z[j] + rest)
+            block = land[p, h, g * Z + j]
             prods[h, s] = product(block, index_s[0, s])[:HV]
             prods[h, s + 1] = product(block, index_s[0, s + 1])[HV:]
-
-        unrolled(per, 4, step)
 
     def add(h, first, count):
         def step(i, total):
@@ -168,10 +156,14 @@
         lax.fori_loop(0, count // 8, step, jnp.zeros((HV, 256), F32))
 
     def apply(p, h):
-        for g in range(CH):
+        def step(g, carry):
             received_products(p, h, g)
-            if g == CH // 2 - 1:
-                add(h, 0, nb + n)
+            return carry
+
+        lax.fori_loop(0, groups // 2, step, 0)
+        add(h, 0, nb + n)
+        lax.fori_loop(groups // 2, groups - 1, step, 0)
+        received_products(p, h, groups - 1, Z - 1)
         add(h, nb + n, n)
 
     def summed(r):
@@ -214,7 +206,7 @@
         return jnp.sum(jnp.where(where, value, 0), axis=0, keepdims=True)
 
     src = src_ref[...]
-    late = (src >= nb) & (lax.rem(lax.div(src - nb, 2), C) != c)
+    late = (src >= nb) & (lax.rem(lax.div(src - nb, 2), C) == c)
     row = row_ref[...] + jnp.where(late, nb, 0)
     row_c, src_c = upright(row), upright(src)
     key = row * nt + lax.broadcasted_iota(jnp.int32, (1, nt), 1)
@@ -333,13 +325,13 @@
         unrolled(nb // 2, 4, step)
 
     sums = sums.reshape(4, 2, HV, wide)
-    odd = lax.rem(lax.div(lax.broadcasted_iota(jnp.int32, (4, HV, wide), 2), 8), 2) == 1
-    sums = jnp.where(odd, sums[:, 1], sums[:, 0]).reshape(4 * HV, wide)
-    picked = lax.dot_general(
-        sums, jnp.where(matches, 1.0, 0.0).astype(F32), (((1,), (1,)), ((), ())),
-        precision=lax.Precision.HIGHEST, preferred_element_type=F32,
+    even, odd = sums[:, 0].reshape(4 * HV, wide), sums[:, 1].reshape(4 * HV, wide)
+    first = lax.rem(lax.div(lax.broadcasted_iota(jnp.int32, (2 * HV, wide), 1), HV), 2) == 0
+    mine = jnp.where(
+        first,
+        even[: 2 * HV] + pltpu.roll(odd[: 2 * HV], wide - HV, 1),
+        odd[2 * HV :] + pltpu.roll(even[2 * HV :], HV, 1),
     )
-    mine = jnp.concatenate([picked[: 2 * HV], picked[2 * HV :]], axis=1)
 
     def reduce(stage, red, mine, position, count, to, meanwhile):
         red[position] = mine
@@ -371,7 +363,7 @@
     sums_ref[...] = mine
     for p in range(3):
         for h in (0, 1):
-            sent(p, h)
+            many(p, h, 0, 0, n - 1).wait_send()
     for h in (0, 1):
         for d in range(1, ny):
             across(h, d).wait_send()
@@ -387,9 +379,16 @@
     ]
     for copy in copies:
         copy.start()
-    k = gram_ref.shape[1]
-    gram_ref[...] = sums_ref[:, :k]
-    projected_ref[...] = sums_ref[:, k:]
+    wide, k = sums_ref.shape[1], gram_ref.shape[1]
+    column = lax.broadcasted_iota(jnp.int32, (wide, k), 0)
+    vector = lax.broadcasted_iota(jnp.int32, (wide, k), 1)
+    place = lax.div(column, 2 * HV) * HV + lax.rem(column, HV) == vector
+    parity = lax.rem(lax.div(column, HV), 2)
+    for q, out_ref in ((0, gram_ref), (1, projected_ref)):
+        out_ref[...] = jnp.dot(
+            sums_ref[...], jnp.where(place & (parity == q), 1.0, 0.0).astype(F32),
+            precision=lax.Precision.HIGHEST, preferred_element_type=F32,
+        )
     for copy in copies:
         copy.wait()
 
@@ -401,7 +400,6 @@
         nt = tile_vals.shape[0]
         nb = vectors.shape[1] // 256
         k = ritz.shape[0]
-        smem = pl.BlockSpec(memory_space=pltpu.SMEM)
         vmem = pl.BlockSpec(memory_space=pltpu.VMEM)
         dma = pltpu.SemaphoreType.DMA
         anywhere = pl.BlockSpec(memory_space=pl.ANY)
@@ -411,9 +409,13 @@
                 pltpu.VMEM(vectors.shape, BF16),
                 pltpu.VMEM((2 * HV, 2 * k), F32),
             ),
-            in_specs=[vmem, vmem, smem, vmem, anywhere, anywhere],
+            in_specs=[anywhere] * 6,
             out_specs=(vmem, vmem),
             scratch_shapes=[
+                pltpu.VMEM(tile_row.shape, jnp.int32),
+                pltpu.VMEM(tile_src.shape, jnp.int32),
+                pltpu.SMEM(send_list.shape[::-1], jnp.int32),
+                pltpu.VMEM(ritz.shape[::-1], BF16),
                 pltpu.VMEM(vectors.shape, BF16),
                 pltpu.VMEM((nt, 256, 256), BF16),
                 pltpu.VMEM((2, 2, nb, HV, 256), F32),
@@ -429,11 +431,12 @@
                 pltpu.VMEM((8, 256), F32),
                 pltpu.SMEM((8, 256), jnp.int32),
                 pltpu.SMEM((8, 256), F32),
+                dma((4,)),
                 dma,
                 dma((2,)),
                 dma((8,)),
                 dma((3, 2)),
-                dma((3, 2, CH)),
+                dma((3, 2, X * C)),
                 dma((2, ny - 1)),
                 dma((2, ny - 1)),
                 dma((2, 7)),

time: 97.4 us -> 94.6 us (0.971)
  Pallas kernels: 96.6 us -> 93.9 us
    pallas_call x1, Pallas kernels: 95.2 us -> 92.5 us  [body(): pl.pallas_call(functools.partial(kernel, n, ny, nb, nt, vectors.shape[1]...]
where the time goes in v3:
time: 94.6 us; the launch traced here: 94.5 us
  Pallas kernels  93.9 us (99%)
    pallas_call x1, Pallas kernels, body(): pl.pallas_call(functools.partial(kernel, n, ny, nb, nt, vectors.shape[1]...  92.5 us

profile of v3, /device:TPU:1, one launch (start us, length us, event | category | flops | bytes accessed | tf_op | source)
XLA Modules:
  0.0 94.5 jit_solution(11674015637428650144)
XLA Ops:
  0.6 92.5 %shard_map.85 = (bf16[16,16384]{1,0:T(8,128)(2,1)S(1)}, f32[16,128]{1,0:T(8,128)S(1)}) custom-call(s32[1,192]{1,0:T(1,128)} %row_hbm.1, s32[1,192]{1,0:T(1,128)} %src_hbm.1, s32[2,64]{1,0:T(2,128)} %bitcast.3, bf16[16,64]{1,0:T(8,128)(2,1)} %bitcast.2, bf16[16,16384]{1,0:T(8,128)(2,1)} %vec_hbm.1, bf16[192,256,256]{2,1,0:T(8,128)(2,1)} %tiles_hbm.1), custom_call_target="tpu_custom_call" | custom-call | tf_op jit(solution)/shard_map/pallas_call | solution.py:406
  93.1 1.4 %shard_map.86 = (bf16[16,16384]{1,0:T(8,128)(2,1)}, f32[16,64]{1,0:T(8,128)}, f32[16,64]{1,0:T(8,128)}) custom-call(bf16[16,16384]{1,0:T(8,128)(2,1)S(1)} %get-tuple-element.5.rot_ref, f32[16,128]{1,0:T(8,128)S(1)} %get-tuple-element.6.sums_ref), custom_call_target="tpu_custom_call" | custom-call | tf_op jit(solution)/shard_map/pallas_call | solution.py:449

commit v4 on v3

--- a/solution.py
+++ b/solution.py
@@ -369,7 +369,7 @@
             across(h, d).wait_send()
 
 
-def finish(rot_ref, sums_ref, rotated_hbm, gram_ref, projected_ref, sem):
+def finish(rot_ref, sums_ref, rotated_hbm, gram_hbm, projected_hbm, gram_ref, projected_ref, sem, out_sem):
     rows = rot_ref.shape[1] // sem.shape[0]
     copies = [
         pltpu.make_async_copy(
@@ -389,6 +389,9 @@
             sums_ref[...], jnp.where(place & (parity == q), 1.0, 0.0).astype(F32),
             precision=lax.Precision.HIGHEST, preferred_element_type=F32,
         )
+    for i, (a, b) in enumerate(((gram_ref, gram_hbm), (projected_ref, projected_hbm))):
+        copies.append(pltpu.make_async_copy(a, b, out_sem.at[i]))
+        copies[-1].start()
     for copy in copies:
         copy.wait()
 
@@ -454,8 +457,13 @@
                 jax.ShapeDtypeStruct((2 * HV, k), F32),
             ),
             in_specs=[vmem, vmem],
-            out_specs=(anywhere, vmem, vmem),
-            scratch_shapes=[dma((4,))],
+            out_specs=(anywhere, anywhere, anywhere),
+            scratch_shapes=[
+                pltpu.VMEM((2 * HV, k), F32),
+                pltpu.VMEM((2 * HV, k), F32),
+                dma((4,)),
+                dma((2,)),
+            ],
             compiler_params=pltpu.CompilerParams(vmem_limit_bytes=4 << 20),
         )(rotated, sums)
 

time: 94.6 us -> 94.1 us (level)
  no operation moved by 1% of the time
where the time goes in v4:
time: 94.1 us; the launch traced here: 94 us
  Pallas kernels  93.4 us (99%)
    pallas_call x1, Pallas kernels, body(): pl.pallas_call(functools.partial(kernel, n, ny, nb, nt, vectors.shape[1]...  92.5 us

profile of v4, /device:TPU:1, one launch (start us, length us, event | category | flops | bytes accessed | tf_op | source)
XLA Modules:
  0.0 94.0 jit_solution(18243418551414820517)
XLA Ops:
  0.6 92.5 %shard_map.85 = (bf16[16,16384]{1,0:T(8,128)(2,1)S(1)}, f32[16,128]{1,0:T(8,128)S(1)}) custom-call(s32[1,192]{1,0:T(1,128)} %row_hbm.1, s32[1,192]{1,0:T(1,128)} %src_hbm.1, s32[2,64]{1,0:T(2,128)} %bitcast.3, bf16[16,64]{1,0:T(8,128)(2,1)} %bitcast.2, bf16[16,16384]{1,0:T(8,128)(2,1)} %vec_hbm.1, bf16[192,256,256]{2,1,0:T(8,128)(2,1)} %tiles_hbm.1), custom_call_target="tpu_custom_call" | custom-call | tf_op jit(solution)/shard_map/pallas_call | solution.py:409
  93.1 0.9 shard_map.86

commit v5 on v4

--- a/solution.py
+++ b/solution.py
@@ -103,6 +103,7 @@
 
         def step(k, dest):
             outb[p, h, k] = chosen(side, h, dest)
+            message(p, h, k, dest).start()
 
         each_peer(step)
 
@@ -112,9 +113,6 @@
             send_sem=ssem.at[p, h], recv_sem=rsem.at[p, h, lax.div(k, Z)],
             device_id={"rows": dest}, device_id_type=MESH,
         )
-
-    def send(p, h):
-        each_peer(lambda k, dest: message(p, h, k, dest).start())
 
     def many(p, h, g, first, count):
         at = pl.ds(first, count)
@@ -188,11 +186,9 @@
         )
 
     accs[nt] = jnp.zeros((HV, 256), F32)
+    pl.semaphore_wait(barrier, n - 1 + ny - 1)
     pack(0, 0)
-    pl.semaphore_wait(barrier, n - 1 + ny - 1)
-    send(0, 0)
     pack(0, 1)
-    send(0, 1)
 
     side = (nt, nt)
     down = lax.broadcasted_iota(jnp.int32, side, 0)
@@ -270,7 +266,6 @@
             apply(p, h)
             pairs(maker(h))
             pack(p + 1, h)
-            send(p + 1, h)
             if p == 1:
                 for d in range(1, ny):
                     across(h, d).start()
@@ -309,11 +304,11 @@
             rest = jnp.concatenate([summed(2 * i), summed(2 * i + 1)], axis=0).astype(BF16)
             rows = jnp.concatenate([full[cy, 0, i], full[cy, 1, i], opb[i], rest], axis=0)
             total = total + lax.dot_general(
-                rows, weights(i), (((1,), (1,)), ((), ())), preferred_element_type=F32
+                weights(i), rows, (((1,), (1,)), ((), ())), preferred_element_type=F32
             )
         return total
 
-    sums = lax.fori_loop(0, nb // 8, contract, jnp.zeros((8 * HV, wide), F32))
+    sums = lax.fori_loop(0, nb // 8, contract, jnp.zeros((wide, 8 * HV), F32)).T
 
     def rotate():
         def step(i):
@@ -357,8 +352,8 @@
 
     plane = X * C
     spot = lax.rem(me, plane)
-    mine = reduce(0, red1, mine, spot, plane, lambda d: z * plane + lax.rem(spot + d, plane), rotate)
-    mine = reduce(1, red2, mine, z, Z, lambda d: lax.rem(z + d, Z) * plane + spot, lambda: None)
+    mine = reduce(0, red1, mine, spot, plane, lambda d: z * plane + lax.rem(spot + d, plane), lambda: None)
+    mine = reduce(1, red2, mine, z, Z, lambda d: lax.rem(z + d, Z) * plane + spot, rotate)
     mine = mine * (1.0 / total_nodes)
     sums_ref[...] = mine
     for p in range(3):

time: 94.1 us -> 94.3 us (level)
  no operation moved by 1% of the time
where the time goes in v5:
time: 94.3 us; the launch traced here: 94.2 us
  Pallas kernels  93.5 us (99%)
    pallas_call x1, Pallas kernels, body(): pl.pallas_call(functools.partial(kernel, n, ny, nb, nt, vectors.shape[1]...  92.7 us

profile of v5, /device:TPU:1, one launch (start us, length us, event | category | flops | bytes accessed | tf_op | source)
XLA Modules:
  0.0 94.2 jit_solution(19455904951985499)
XLA Ops:
  0.6 92.7 %shard_map.85 = (bf16[16,16384]{1,0:T(8,128)(2,1)S(1)}, f32[16,128]{1,0:T(8,128)S(1)}) custom-call(s32[1,192]{1,0:T(1,128)} %row_hbm.1, s32[1,192]{1,0:T(1,128)} %src_hbm.1, s32[2,64]{1,0:T(2,128)} %bitcast.3, bf16[16,64]{1,0:T(8,128)(2,1)} %bitcast.2, bf16[16,16384]{1,0:T(8,128)(2,1)} %vec_hbm.1, bf16[192,256,256]{2,1,0:T(8,128)(2,1)} %tiles_hbm.1), custom_call_target="tpu_custom_call" | custom-call | tf_op jit(solution)/shard_map/pallas_call | solution.py:404
  93.3 0.9 shard_map.86
